TPU v7x, 32 devices: a whole 2x2x4 slice. The times are simulated.
32 devices in a mesh: frames: 16 (over z, y, x), atoms: 2 (over core).
Axes of the slice: x: 2, y: 2, z: 4, core: 2. Of those that a mesh axis runs over, the one named last changes fastest.
Arguments:
- displacements: float32 [1024, 3, 4096], P('frames', None, 'atoms'), may hold values from -2 to 2
Outputs:
- msd: float32 [4096, 1024], P(('atoms', 'frames'))
All inputs are finite; a program needn't handle non-finite values.
Results may differ from a plain program's by a relative error of at most 0.0003.
Values sent between devices are 32-bit elements; how exact they have to be, the bound alone decides.
A program may use at most 64 MiB of HBM per device.

v0:
```python
import math

import jax
import jax.numpy as jnp
from jax import lax
from jax.sharding import PartitionSpec as P


def carried_in(array, axis, combine, identity):
    count, index = (lax.axis_size(axis), lax.axis_index(axis))
    everything = lax.all_gather(array, axis)
    start = jnp.broadcast_to(jnp.asarray(identity, array.dtype), array.shape)

    def hop(k, before):
        reached = k < index
        new = combine(before, everything[k])
        return jnp.where(reached, new, before)

    return lax.fori_loop(0, count, hop, start)


def lag_table(positions):
    length = positions.shape[0]
    count = positions.shape[3]
    series = positions.reshape(length, 3 * count)
    squares = jnp.sum(positions * positions, axis=(1, 2))
    zero_row = jnp.zeros((1, count), jnp.float32)
    running = jnp.concatenate([zero_row, jnp.cumsum(squares, axis=0)], axis=0)
    head = running[length][None, :] - running[:length]
    tail = jnp.flip(running[1:], 0)
    block = min(256, length)
    frame = jnp.arange(length, dtype=jnp.int32)
    starts = jnp.arange(0, length, block, dtype=jnp.int32)

    def add_block(corr, start):
        freq = start + jnp.arange(block, dtype=jnp.int32)
        phase = frame[:, None] * freq[None, :] % (2 * length)
        angle = phase.astype(jnp.float32) * (math.pi / length)
        cosine = jnp.cos(angle)
        sine = jnp.sin(angle)
        real_part = lax.dot_general(
            series, cosine, (((0,), (0,)), ((), ())), precision=lax.Precision.HIGHEST
        )
        imag_part = lax.dot_general(
            series, sine, (((0,), (0,)), ((), ())), precision=lax.Precision.HIGHEST
        )
        power = jnp.sum(
            (real_part * real_part + imag_part * imag_part).reshape(3, count, block), axis=0
        )
        weight = jnp.where(freq == 0, 1.0, 2.0).astype(jnp.float32) / (2.0 * length)
        term = lax.dot_general(
            power * weight[None, :],
            cosine,
            (((1,), (1,)), ((), ())),
            precision=lax.Precision.HIGHEST,
        )
        return (corr + term, None)

    corr, _ = lax.scan(add_block, jnp.zeros((count, length), jnp.float32), starts)
    parity = jnp.where(frame % 2 == 0, 1.0, -1.0).astype(jnp.float32)
    highest = jnp.dot(parity, series, precision=lax.Precision.HIGHEST)
    power_top = jnp.sum((highest * highest).reshape(3, count), axis=0)
    corr = corr + power_top[:, None] * parity[None, :] / (2.0 * length)
    counts = (length - frame).astype(jnp.float32)
    return (jnp.transpose(head + tail) - 2.0 * corr) / counts[None, :]


def add_carry(earlier, later):
    return earlier + later


def per_device(displacements):
    local_frames, _, atom_count = displacements.shape
    groups = lax.axis_size("frames")
    atom_total = atom_count * lax.axis_size("atoms")
    summed = lax.psum(jnp.sum(displacements, axis=2), "atoms")
    centred = displacements - (summed / atom_total)[:, :, None]
    partial_value = jnp.cumsum(centred, axis=0)
    earlier = carried_in(partial_value[-1], "frames", add_carry, jnp.zeros_like(partial_value[-1]))
    positions = (partial_value + earlier[None]).reshape(
        local_frames, 3, groups, atom_count // groups
    )
    return lag_table(lax.all_to_all(positions, "frames", split_axis=2, concat_axis=0, tiled=True))


def solution(mesh):
    placed = (P("frames", None, "atoms"),)
    return jax.shard_map(
        per_device,
        mesh=mesh,
        in_specs=placed,
        out_specs=P(("atoms", "frames"), None),
        check_vma=False,
    )
```

profile of v0, /device:TPU:0, one launch (start us, length us, event | category | flops | bytes accessed | tf_op | source)
XLA Modules:
  0.0 185.2 jit_solution(4736972818235027603)
XLA Ops:
  0.0 1.7 reduce_sum.41
  1.7 2.6 %psum.7 = f32[64,3]{0,1:T(4,128)S(1)} all-reduce(f32[64,3]{0,1:T(4,128)S(1)} %reduce_sum.41), channel_id=1, replica_groups=mesh['frames'=16,'atoms'=2] {'atoms'}, use_global_device_ids=true, to_apply=%region_1.0 | all-reduce | flops 192 | bytes 1536 | tf_op jit(solution)/shard_map/psum | solution.py:76
  5.5 2.0 %reshape.67 = f32[64,3,16,128]{3,2,1,0:T(8,128)} reshape(f32[64,3,2048]{2,1,0:T(4,128)S(1)} %fusion.30) | data formatting | bytes 3145728 | tf_op jit(solution)/shard_map/jit(cumsum)/reduce_window_sum | solution.py:78
  7.6 45.4 %all_gather.3 = f32[16,3,2048]{2,1,0:T(4,128)S(1)} all-gather(f32[1,3,2048]{2,1,0:T(4,128)S(1)} %slice.20), channel_id=1, replica_groups=mesh['frames'=16,'atoms'=2] {'frames'}, dimensions={0}, use_global_device_ids=true | all-gather | bytes 417792 | tf_op jit(solution)/shard_map/all_gather | solution.py:11
  53.8 1.5 copy_add_fusion
  55.3 1.6 copy.36
  57.0 3.9 %all-to-all-start = ((f32[64,3,16,128]{3,0,1,2:T(8,128)}), f32[64,3,16,128]{3,0,1,2:T(8,128)S(1)}, u32[]{:S(2)}, u32[]{:S(2)}) async-start(f32[64,3,16,128]{3,0,1,2:T(8,128)} %copy.36), calls=%async_computation | async-start | bytes 3145728 | tf_op jit(solution)/shard_map/all_to_all | solution.py:83
  61.4 29.4 %all-to-all-done = f32[64,3,16,128]{3,0,1,2:T(8,128)S(1)} async-done(((f32[64,3,16,128]{3,0,1,2:T(8,128)}), f32[64,3,16,128]{3,0,1,2:T(8,128)S(1)}, u32[]{:S(2)}, u32[]{:S(2)}) %all-to-all-start) | async-done | bytes 1572896 | tf_op jit(solution)/shard_map/all_to_all | solution.py:83
  93.9 88.8 %while.28 = (s32[]{:T(128)}, f32[128,1024]{1,0:T(8,128)}, s32[4]{0:T(128)}, f32[1024,384]{1,0:T(8,128)S(1)}, s32[]{:T(128)}, /*index=5*/s32[]{:T(128)}, f32[]{:T(128)}) while((s32[]{:T(128)}, f32[128,1024]{1,0:T(8,128)}, s32[4]{0:T(128)}, f32[1024,384]{1,0:T(8,128)S(1)}, s32[]{:T(128)}, /*index=5*/s32[]{:T(128)}, ...), condition=%wide.region_10.11_spmd.clone, body=%wide.region_8.10_spmd.clone.sunk | while | flops 2830238976 | bytes 6826123 | solution.py:59
  93.9 1.2 dynamic_slice.20
  95.7 6.3 %convolution_multiply_fusion.3 = f32[256,384]{1,0:T(8,128)S(1)} fusion(f32[1024,384]{1,0:T(8,128)S(1)} %get-tuple-element.285, s32[256]{0:T(256)S(1)} %iota_add_fusion.2), kind=kOutput, calls=%fused_computation.5.clone.1 | convolution fusion | flops 1211727872 | bytes 1967104 | tf_op jit(solution)/shard_map/while/body/eval_jaxpr/dot_general | solution.py:44
  102.0 6.3 %fusion.62 = f32[384,256]{0,1:T(8,128)S(1)} fusion(f32[256,384]{1,0:T(8,128)S(1)} %convolution_multiply_fusion.3, f32[1024,384]{1,0:T(8,128)S(1)} %get-tuple-element.285, s32[256]{0:T(256)S(1)} %iota_add_fusion.2), kind=kOutput, calls=%fused_computation.9.clone.1 | convolution fusion | flops 1211826176 | bytes 2360320 | tf_op jit(solution)/shard_map/while/body/eval_jaxpr/dot_general | solution.py:41
  109.1 6.8 %convolution_add_fusion.2 = f32[128,1024]{1,0:T(8,128)} fusion(f32[128,1024]{1,0:T(8,128)} %get-tuple-element.276, s32[256]{0:T(256)} %copy-done.1, pred[]{:T(512)S(6)} %compare.11, f32[128,256]{1,0:T(8,128)S(1)} %reduce_sum.49, f32[256]{0:T(256)S(1)} %fusion.63), kind=kOutput, calls=%fused_computation.7.clone.1 | convolution fusion | flops 406618112 | bytes 1181697 | tf_op jit(solution)/shard_map/while/body/eval_jaxpr/dot_general | solution.py:51
  117.7 6.3 %convolution_multiply_fusion.3 = f32[256,384]{1,0:T(8,128)S(1)} fusion(f32[1024,384]{1,0:T(8,128)S(1)} %get-tuple-element.285, s32[256]{0:T(256)S(1)} %iota_add_fusion.2), kind=kOutput, calls=%fused_computation.5.clone.1 | convolution fusion | flops 1211727872 | bytes 1967104 | tf_op jit(solution)/shard_map/while/body/eval_jaxpr/dot_general | solution.py:44
  124.0 6.3 %fusion.62 = f32[384,256]{0,1:T(8,128)S(1)} fusion(f32[256,384]{1,0:T(8,128)S(1)} %convolution_multiply_fusion.3, f32[1024,384]{1,0:T(8,128)S(1)} %get-tuple-element.285, s32[256]{0:T(256)S(1)} %iota_add_fusion.2), kind=kOutput, calls=%fused_computation.9.clone.1 | convolution fusion | flops 1211826176 | bytes 2360320 | tf_op jit(solution)/shard_map/while/body/eval_jaxpr/dot_general | solution.py:41
  131.1 7.0 %convolution_add_fusion.2 = f32[128,1024]{1,0:T(8,128)} fusion(f32[128,1024]{1,0:T(8,128)} %get-tuple-element.276, s32[256]{0:T(256)} %copy-done.1, pred[]{:T(512)S(6)} %compare.11, f32[128,256]{1,0:T(8,128)S(1)} %reduce_sum.49, f32[256]{0:T(256)S(1)} %fusion.63), kind=kOutput, calls=%fused_computation.7.clone.1 | convolution fusion | flops 406618112 | bytes 1181697 | tf_op jit(solution)/shard_map/while/body/eval_jaxpr/dot_general | solution.py:51
  138.2 1.2 dynamic_slice.20
  139.9 6.3 %convolution_multiply_fusion.3 = f32[256,384]{1,0:T(8,128)S(1)} fusion(f32[1024,384]{1,0:T(8,128)S(1)} %get-tuple-element.285, s32[256]{0:T(256)S(1)} %iota_add_fusion.2), kind=kOutput, calls=%fused_computation.5.clone.1 | convolution fusion | flops 1211727872 | bytes 1967104 | tf_op jit(solution)/shard_map/while/body/eval_jaxpr/dot_general | solution.py:44
  146.3 6.3 %fusion.62 = f32[384,256]{0,1:T(8,128)S(1)} fusion(f32[256,384]{1,0:T(8,128)S(1)} %convolution_multiply_fusion.3, f32[1024,384]{1,0:T(8,128)S(1)} %get-tuple-element.285, s32[256]{0:T(256)S(1)} %iota_add_fusion.2), kind=kOutput, calls=%fused_computation.9.clone.1 | convolution fusion | flops 1211826176 | bytes 2360320 | tf_op jit(solution)/shard_map/while/body/eval_jaxpr/dot_general | solution.py:41
  153.4 7.0 %convolution_add_fusion.2 = f32[128,1024]{1,0:T(8,128)} fusion(f32[128,1024]{1,0:T(8,128)} %get-tuple-element.276, s32[256]{0:T(256)} %copy-done.1, pred[]{:T(512)S(6)} %compare.11, f32[128,256]{1,0:T(8,128)S(1)} %reduce_sum.49, f32[256]{0:T(256)S(1)} %fusion.63), kind=kOutput, calls=%fused_computation.7.clone.1 | convolution fusion | flops 406618112 | bytes 1181697 | tf_op jit(solution)/shard_map/while/body/eval_jaxpr/dot_general | solution.py:51
  162.2 6.3 %convolution_multiply_fusion.3 = f32[256,384]{1,0:T(8,128)S(1)} fusion(f32[1024,384]{1,0:T(8,128)S(1)} %get-tuple-element.285, s32[256]{0:T(256)S(1)} %iota_add_fusion.2), kind=kOutput, calls=%fused_computation.5.clone.1 | convolution fusion | flops 1211727872 | bytes 1967104 | tf_op jit(solution)/shard_map/while/body/eval_jaxpr/dot_general | solution.py:44
  168.5 6.3 %fusion.62 = f32[384,256]{0,1:T(8,128)S(1)} fusion(f32[256,384]{1,0:T(8,128)S(1)} %convolution_multiply_fusion.3, f32[1024,384]{1,0:T(8,128)S(1)} %get-tuple-element.285, s32[256]{0:T(256)S(1)} %iota_add_fusion.2), kind=kOutput, calls=%fused_computation.9.clone.1 | convolution fusion | flops 1211826176 | bytes 2360320 | tf_op jit(solution)/shard_map/while/body/eval_jaxpr/dot_general | solution.py:41
  175.6 7.0 %convolution_add_fusion.2 = f32[128,1024]{1,0:T(8,128)} fusion(f32[128,1024]{1,0:T(8,128)} %get-tuple-element.276, s32[256]{0:T(256)} %copy-done.1, pred[]{:T(512)S(6)} %compare.11, f32[128,256]{1,0:T(8,128)S(1)} %reduce_sum.49, f32[256]{0:T(256)S(1)} %fusion.63), kind=kOutput, calls=%fused_computation.7.clone.1 | convolution fusion | flops 406618112 | bytes 1181697 | tf_op jit(solution)/shard_map/while/body/eval_jaxpr/dot_general | solution.py:51
  182.6 1.2 copy.42
  (70 shorter events, 15.0 us)
Async XLA Ops:
  0.0 4.3 %copy-start = (f32[64,3,2048]{2,0,1:T(8,128)S(1)}, f32[64,3,2048]{2,0,1:T(8,128)}, u32[]{:S(2)}) copy-start(f32[64,3,2048]{2,0,1:T(8,128)} %param.5) | copy-start | bytes 4718596
  57.0 33.8 %all-to-all-start = ((f32[64,3,16,128]{3,0,1,2:T(8,128)}), f32[64,3,16,128]{3,0,1,2:T(8,128)S(1)}, u32[]{:S(2)}, u32[]{:S(2)}) async-start(f32[64,3,16,128]{3,0,1,2:T(8,128)} %copy.36), calls=%async_computation | async-start | bytes 3145728 | tf_op jit(solution)/shard_map/all_to_all | solution.py:83
  95.7 6.4 %copy-start.1 = (s32[256]{0:T(256)}, s32[256]{0:T(256)S(1)}, u32[]{:S(2)}) copy-start(s32[256]{0:T(256)S(1)} %iota_add_fusion.2) | copy-start | bytes 3076 | tf_op jit(solution)/shard_map/while
  117.7 6.4 %copy-start.1 = (s32[256]{0:T(256)}, s32[256]{0:T(256)S(1)}, u32[]{:S(2)}) copy-start(s32[256]{0:T(256)S(1)} %iota_add_fusion.2) | copy-start | bytes 3076 | tf_op jit(solution)/shard_map/while
  139.9 6.4 %copy-start.1 = (s32[256]{0:T(256)}, s32[256]{0:T(256)S(1)}, u32[]{:S(2)}) copy-start(s32[256]{0:T(256)S(1)} %iota_add_fusion.2) | copy-start | bytes 3076 | tf_op jit(solution)/shard_map/while
  162.2 6.4 %copy-start.1 = (s32[256]{0:T(256)}, s32[256]{0:T(256)S(1)}, u32[]{:S(2)}) copy-start(s32[256]{0:T(256)S(1)} %iota_add_fusion.2) | copy-start | bytes 3076 | tf_op jit(solution)/shard_map/while
where the time goes:
time: 186 us; the launch traced here: 185 us
  matrix products  79.3 us (43%)
  blocking collectives  48 us (26%)
  waiting for transfers between devices  29.4 us (16%)
  local copies, waits for them, and re-layouts  12.9 us (7%)
  other arithmetic  10.9 us (6%)
  starting transfers between devices  3.89 us (2%)
    all_gather x1, blocking collectives, carried_in(): everything = lax.all_gather(array, axis)  45.4 us
    all_to_all x1, waiting for transfers between devices, per_device(): lax.all_to_all(positions, 'frames', split_axis=2, concat_axis=0, tiled=True)  29.4 us
    dot_general x4, matrix products, add_block(): lax.dot_general(power * weight[None, :], cosine, (((1,), (1,)), ((), ()))...  27.9 us
    dot_general x4, matrix products, add_block(): lax.dot_general(series, sine, (((0,), (0,)), ((), ())), precision=lax.Pre...  25.3 us
    dot_general x4, matrix products, add_block(): lax.dot_general(series, cosine, (((0,), (0,)), ((), ())), precision=lax.P...  25.2 us
    dynamic_slice x4, local copies, waits for them, and re-layouts, lag_table(): lax.scan(add_block, jnp.zeros((count, length), jnp.float32), starts)  4.83 us
    all_to_all x1, starting transfers between devices, per_device(): lax.all_to_all(positions, 'frames', split_axis=2, concat_axis=0, tiled=True)  3.89 us
  transfers between devices with their start and end apart: 1, of which 1 were waited for; matrix products, arithmetic and copies ran while one was open for 0% of the time, Pallas kernels for 0%

commit v1 on v0

--- a/solution.py
+++ b/solution.py
@@ -1,9 +1,19 @@
+import functools
 import math
 
 import jax
 import jax.numpy as jnp
+import ml_dtypes
+import numpy as np
 from jax import lax
+from jax.experimental import pallas as pl
+from jax.experimental.pallas import tpu as pltpu
 from jax.sharding import PartitionSpec as P
+
+
+BLOCK = 256
+LANES = 128
+MESH = pl.DeviceIdType.MESH
 
 
 def carried_in(array, axis, combine, identity):
@@ -83,12 +93,321 @@
     return lag_table(lax.all_to_all(positions, "frames", split_axis=2, concat_axis=0, tiled=True))
 
 
+def tables():
+    points = 2 * BLOCK
+    index = np.arange(BLOCK)
+    angle = 2.0 * np.pi * (np.outer(index, index) % points) / points
+    forward = np.zeros((points + 16, BLOCK))
+    forward[:BLOCK] = np.cos(angle)
+    forward[BLOCK:points] = -np.sin(angle)
+    forward[points] = 1.0 - 2.0 * (index % 2)
+    high = forward.astype(ml_dtypes.bfloat16)
+    low = (forward - high.astype(np.float64)).astype(ml_dtypes.bfloat16)
+    weight = np.where(index == 0, 1.0, 2.0)[None, :] / points
+    inverse = np.concatenate([np.cos(angle) * weight, -np.sin(angle) * weight], axis=1)
+    row, col = index[:, None], index[None, :]
+    sums = np.stack([col <= row, col >= row, col <= BLOCK - 1 - row])
+    return (
+        np.stack([high, low]),
+        sums.astype(ml_dtypes.bfloat16),
+        (-2.0 * inverse).astype(np.float32),
+    )
+
+
+def split(value, terms):
+    parts = []
+    for _ in range(terms - 1):
+        part = value.astype(jnp.bfloat16)
+        parts.append(part)
+        value = value - part.astype(jnp.float32)
+    return parts + [value.astype(jnp.bfloat16)]
+
+
+def mm(a, b):
+    return jnp.dot(a, b, preferred_element_type=jnp.float32)
+
+
+def kernel(
+    groups, atom_total, x, forward, sums, inverse, out,
+    xv, recv, mine, sibling, total, msgs, fv, sv, iv, drift, spectrum, acc_re, acc_im, acc_top, squares,
+    load_sem, const_sem, own_sem, send_sem, recv_sem, pair_send, pair_recv, msg_send, msg_recv,
+):
+    me, core = lax.axis_index("frames"), lax.axis_index("atoms")
+    frames = x.shape[1]
+    width = recv.shape[2]
+    blocks = recv.shape[1] // BLOCK
+    tiles = x.shape[2] // LANES
+
+    loads = [pltpu.make_async_copy(x.at[c], xv.at[c], load_sem.at[c]) for c in range(3)]
+    for load in loads:
+        load.start()
+    consts = [
+        pltpu.make_async_copy(src, dst, const_sem.at[i])
+        for i, (src, dst) in enumerate(((forward, fv), (sums, sv), (inverse, iv)))
+    ]
+    for const in consts:
+        const.start()
+
+    def peer_at(k):
+        return lax.rem(me + k, groups)
+
+    def own_copy(c):
+        return pltpu.make_async_copy(
+            x.at[c, :, pl.ds(pl.multiple_of(me * width, width), width)],
+            recv.at[c, pl.ds(pl.multiple_of(me * frames, frames), frames), :],
+            own_sem.at[c],
+        )
+
+    barrier = pltpu.get_barrier_semaphore()
+
+    def greet(k, carry):
+        pl.semaphore_signal(barrier, inc=1, device_id={"frames": peer_at(k)}, device_id_type=MESH)
+        return carry
+
+    pl.semaphore_signal(barrier, inc=1, device_id={"atoms": 1 - core}, device_id_type=MESH)
+    lax.fori_loop(1, groups, greet, 0)
+    pl.semaphore_wait(barrier, groups)
+
+    def far_first(t):
+        return groups // 2 + (1 - 2 * lax.rem(t, 2)) * ((t + 1) // 2)
+
+    def send_component(c):
+        def send(t, carry):
+            peer = peer_at(far_first(t))
+            pltpu.make_async_remote_copy(
+                src_ref=x.at[c, :, pl.ds(pl.multiple_of(peer * width, width), width)],
+                dst_ref=recv.at[c, pl.ds(pl.multiple_of(me * frames, frames), frames), :],
+                send_sem=send_sem.at[c],
+                recv_sem=recv_sem.at[c],
+                device_id={"frames": peer},
+                device_id_type=MESH,
+            ).start()
+            return carry
+
+        lax.fori_loop(0, groups - 1, send, 0)
+        own_copy(c).start()
+
+    send_component(0)
+
+    parts = []
+    for c in range(3):
+        loads[c].wait()
+        part = xv[c, :, 0:LANES]
+        for tile in range(1, tiles):
+            part = part + xv[c, :, tile * LANES : (tile + 1) * LANES]
+        parts.append(part)
+    lanes = mine.shape[1]
+    if lanes > 3 * frames:
+        parts.append(jnp.zeros((lanes - 3 * frames, LANES), jnp.float32))
+    mine[...] = jnp.sum(jnp.transpose(jnp.concatenate(parts, axis=0)), axis=0, keepdims=True)
+    pair = pltpu.make_async_remote_copy(
+        src_ref=mine,
+        dst_ref=sibling,
+        send_sem=pair_send,
+        recv_sem=pair_recv,
+        device_id={"atoms": 1 - core},
+        device_id_type=MESH,
+    )
+    pair.start()
+    pair.wait()
+    total[...] = (mine[...] + sibling[...]) / atom_total
+
+    def tell(k):
+        return pltpu.make_async_remote_copy(
+            src_ref=total,
+            dst_ref=msgs.at[me],
+            send_sem=msg_send.at[k],
+            recv_sem=msg_recv.at[k],
+            device_id={"frames": peer_at(k)},
+            device_id_type=MESH,
+        )
+
+    def tell_start(k, carry):
+        tell(k).start()
+        return carry
+
+    lax.fori_loop(1, groups, tell_start, 0)
+    send_component(1)
+    send_component(2)
+    msgs[pl.ds(me, 1)] = total[...][None]
+
+    acc_re[...] = jnp.zeros_like(acc_re)
+    acc_im[...] = jnp.zeros_like(acc_im)
+    acc_top[...] = jnp.zeros_like(acc_top)
+    squares[...] = jnp.zeros_like(squares)
+    for const in consts:
+        const.wait()
+
+    def heard(k, carry):
+        source = lax.rem(me + groups - k, groups)
+        pltpu.make_async_remote_copy(
+            src_ref=total,
+            dst_ref=msgs.at[source],
+            send_sem=msg_send.at[k],
+            recv_sem=msg_recv.at[k],
+            device_id={"frames": source},
+            device_id_type=MESH,
+        ).wait()
+        return carry
+
+    lax.fori_loop(1, groups, heard, 0)
+
+    def spread(b, carry):
+        column = jnp.transpose(jnp.broadcast_to(msgs[pl.ds(b, 1)][0], (LANES, lanes)))
+        for c in range(3):
+            drift[c, pl.ds(pl.multiple_of(b * frames, frames), frames), :] = column[
+                c * frames : (c + 1) * frames
+            ]
+        return carry
+
+    lax.fori_loop(0, groups, spread, 0)
+
+    def lanes_of(value):
+        return [value[:, i * width : (i + 1) * width] for i in range(blocks)]
+
+    def component(c, carry):
+        arrived = recv.at[c, pl.ds(0, (groups - 1) * frames), :]
+        own_copy(c).wait()
+        pltpu.make_async_copy(arrived, arrived, recv_sem.at[c]).wait()
+        centred = jnp.concatenate(
+            [
+                recv[c, i * BLOCK : (i + 1) * BLOCK, :] - drift[c, i * BLOCK : (i + 1) * BLOCK, :]
+                for i in range(blocks)
+            ],
+            axis=1,
+        )
+        high, mid, low = split(centred, 3)
+        running = mm(sv[0], high) + (mm(sv[0], mid) + mm(sv[0], low))
+        before = [jnp.zeros((1, width), jnp.float32)]
+        for last in lanes_of(running[BLOCK - 1 : BLOCK, :])[:-1]:
+            before.append(before[-1] + last)
+        positions = running + jnp.concatenate(before, axis=1)
+        squares[...] += positions * positions
+        high, low = split(positions, 2)
+        spectrum[...] = mm(fv[0], high) + (mm(fv[0], low) + mm(fv[1], high))
+
+        def rows(r, inner):
+            at = pl.ds(pl.multiple_of(r * 8, 8), 8)
+            re = lanes_of(spectrum[at, :])
+            im = lanes_of(spectrum[pl.ds(pl.multiple_of(BLOCK + r * 8, 8), 8), :])
+            for d in range(blocks):
+                here = slice(d * width, (d + 1) * width)
+                real = acc_re[at, here]
+                imag = acc_im[at, here]
+                for i in range(blocks - d):
+                    j = i + d
+                    real = real + (re[i] * re[j] + im[i] * im[j])
+                    if d:
+                        imag = imag + (re[i] * im[j] - im[i] * re[j])
+                acc_re[at, here] = real
+                if d:
+                    acc_im[at, here] = imag
+            return inner
+
+        lax.fori_loop(0, BLOCK // 8, rows, 0, unroll=2)
+        top = lanes_of(spectrum[2 * BLOCK : 2 * BLOCK + 8, :])
+        for d in range(blocks):
+            here = slice(d * width, (d + 1) * width)
+            value = acc_top[:, here]
+            for i in range(blocks - d):
+                value = value + top[i] * top[i + d]
+            acc_top[:, here] = value
+        return carry
+
+    lax.fori_loop(0, 3, component, 0)
+
+    def next_block(value):
+        return jnp.concatenate([value[:, width:], jnp.zeros_like(value[:, :width])], axis=1)
+
+    parity = (1 - 2 * (lax.broadcasted_iota(jnp.int32, (BLOCK, 1), 0) % 2)).astype(jnp.float32)
+    real, imag, top = acc_re[...], acc_im[...], acc_top[0:1, :]
+    cross = jnp.concatenate(
+        [real + parity * next_block(real), imag + parity * next_block(imag)], axis=0
+    )
+    corr = jnp.dot(
+        iv[...], cross, precision=lax.Precision.HIGHEST, preferred_element_type=jnp.float32
+    )
+    corr = corr - (top + next_block(top)) * (parity * (1.0 / BLOCK))
+    parts = split(squares[...], 3)
+    later = mm(sv[1], parts[0]) + (mm(sv[1], parts[1]) + mm(sv[1], parts[2]))
+    parts = [jnp.concatenate(lanes_of(part)[::-1], axis=1) for part in parts]
+    earlier = mm(sv[2], parts[0]) + (mm(sv[2], parts[1]) + mm(sv[2], parts[2]))
+    sums_of = lanes_of(later[0:1, :])
+    whole = []
+    for i in range(blocks):
+        value = jnp.zeros((1, width), jnp.float32)
+        for j in list(range(i + 1, blocks)) + list(range(blocks - 1 - i)):
+            value = value + sums_of[j]
+        whole.append(value)
+    result = later + earlier + jnp.concatenate(whole, axis=1) + corr
+    for i, piece in enumerate(lanes_of(result)):
+        out[:, i * BLOCK : (i + 1) * BLOCK] = jnp.transpose(piece)
+
+    def sent(c, carry):
+        gone = recv.at[c, pl.ds(0, (groups - 1) * frames), :]
+        pltpu.make_async_copy(gone, gone, send_sem.at[c]).wait()
+        return carry
+
+    lax.fori_loop(0, 3, sent, 0)
+
+
+def fused(displacements):
+    frames, _, atom_count = displacements.shape
+    groups = lax.axis_size("frames")
+    length = frames * groups
+    width = atom_count // groups
+    blocks = length // BLOCK
+    forward, sums, inverse = tables()
+    lanes = -(-3 * frames // LANES) * LANES
+    f32, bf16 = jnp.float32, jnp.bfloat16
+    dma = pltpu.SemaphoreType.DMA
+    numerator = pl.pallas_call(
+        functools.partial(kernel, groups, atom_count * lax.axis_size("atoms")),
+        out_shape=jax.ShapeDtypeStruct((width, length), f32),
+        in_specs=[pl.BlockSpec(memory_space=pl.ANY)] * 4,
+        out_specs=pl.BlockSpec(memory_space=pltpu.VMEM),
+        scratch_shapes=[
+            pltpu.VMEM((3, frames, atom_count), f32),
+            pltpu.VMEM((3, length, width), f32),
+            pltpu.VMEM((1, lanes), f32),
+            pltpu.VMEM((1, lanes), f32),
+            pltpu.VMEM((1, lanes), f32),
+            pltpu.VMEM((groups, 1, lanes), f32),
+            pltpu.VMEM(forward.shape, bf16),
+            pltpu.VMEM(sums.shape, bf16),
+            pltpu.VMEM(inverse.shape, f32),
+            pltpu.VMEM((3, length, width), f32),
+            pltpu.VMEM((2 * BLOCK + 16, blocks * width), f32),
+            pltpu.VMEM((BLOCK, blocks * width), f32),
+            pltpu.VMEM((BLOCK, blocks * width), f32),
+            pltpu.VMEM((8, blocks * width), f32),
+            pltpu.VMEM((BLOCK, blocks * width), f32),
+            dma((3,)), dma((3,)), dma((3,)), dma((3,)), dma((3,)),
+            dma, dma, dma((groups,)), dma((groups,)),
+        ],
+        compiler_params=pltpu.CompilerParams(
+            collective_id=0, has_side_effects=True, vmem_limit_bytes=40 * 1024 * 1024
+        ),
+    )(jnp.transpose(displacements, (1, 0, 2)), jnp.asarray(forward), jnp.asarray(sums), jnp.asarray(inverse))
+    counts = (length - jnp.arange(length)).astype(f32)
+    return numerator / counts[None, :]
+
+
+def fits(mesh, shape):
+    groups, pairs = mesh.shape["frames"], mesh.shape["atoms"]
+    length, _, atoms = shape
+    frames = length // groups
+    return pairs == 2 and atoms // (pairs * groups) == LANES and frames % 8 == 0 and length % BLOCK == 0
+
+
 def solution(mesh):
-    placed = (P("frames", None, "atoms"),)
-    return jax.shard_map(
-        per_device,
-        mesh=mesh,
-        in_specs=placed,
-        out_specs=P(("atoms", "frames"), None),
-        check_vma=False,
-    )
+    def run(displacements):
+        return jax.shard_map(
+            fused if fits(mesh, displacements.shape) else per_device,
+            mesh=mesh,
+            in_specs=(P("frames", None, "atoms"),),
+            out_specs=P(("atoms", "frames"), None),
+            check_vma=False,
+        )(displacements)
+
+    return run

time: 186 us -> 50.7 us (0.27)
  matrix products: 79.3 us -> 0 us
  blocking collectives: 48 us -> 0 us
  Pallas kernels: 0 us -> 45 us
  waiting for transfers between devices: 29.4 us -> 0 us
  other arithmetic: 10.9 us -> 0.86 us
  local copies, waits for them, and re-layouts: 12.9 us -> 4.49 us
  starting transfers between devices: 3.89 us -> 0 us
    dot_general x13 -> x0, matrix products: 79.3 us -> none  [the longest x4 27.9 us: add_block(): lax.dot_general(power * weight[None, :], cosine, (((1,), (1,)), ((), ()))...]
    all_gather x1 -> x0, blocking collectives: 45.4 us -> none  [carried_in(): everything = lax.all_gather(array, axis)]
    pallas_call x0 -> x1, Pallas kernels: none -> 45 us  [fused(): pl.pallas_call(functools.partial(kernel, groups, atom_count * lax.axis_si...]
    all_to_all x1 -> x0, waiting for transfers between devices: 29.4 us -> none  [per_device(): lax.all_to_all(positions, 'frames', split_axis=2, concat_axis=0, tiled=True)]
    dynamic_slice x4 -> x0, local copies, waits for them, and re-layouts: 4.83 us -> none  [lag_table(): lax.scan(add_block, jnp.zeros((count, length), jnp.float32), starts)]
    unnamed x4 -> x8, local copies, waits for them, and re-layouts: 0.15 us -> 4.49 us
    all_to_all x1 -> x0, starting transfers between devices: 3.89 us -> none  [per_device(): lax.all_to_all(positions, 'frames', split_axis=2, concat_axis=0, tiled=True)]
    add x5 -> x0, other arithmetic: 3.77 us -> none  [the longest x4 2.24 us: add_block(): freq = start + jnp.arange(block, dtype=jnp.int32)]
  transfers between devices with their start and end apart: 1 -> 0, of which waited for: 1 -> 0; matrix products, arithmetic and copies ran while one was open for 0% -> 0% of each run, Pallas kernels for 0% -> 0%
where the time goes in v1:
time: 50.7 us; the launch traced here: 50.4 us
  Pallas kernels  45 us (89%)
  local copies, waits for them, and re-layouts  4.49 us (9%)
  other arithmetic  0.86 us (2%)
    pallas_call x1, Pallas kernels, fused(): pl.pallas_call(functools.partial(kernel, groups, atom_count * lax.axis_si...  45 us
    unnamed x8, local copies, waits for them, and re-layouts  4.49 us

profile of v1, /device:TPU:0, one launch (start us, length us, event | category | flops | bytes accessed | tf_op | source)
XLA Modules:
  0.0 50.4 jit_solution(10473938306451793969)
XLA Ops:
  0.0 0.0 copy-start
  0.0 1.4 %copy-done = f32[64,3,2048]{2,0,1:T(8,128)S(1)} copy-done((f32[64,3,2048]{2,0,1:T(8,128)S(1)}, f32[64,3,2048]{2,0,1:T(8,128)}, u32[]{:S(2)}) %copy-start) | copy-done | bytes 1572888
  1.4 0.0 copy-start.1
  1.4 1.0 %copy-done.1 = bf16[2,528,256]{2,1,0:T(8,128)(2,1)S(1)} copy-done((bf16[2,528,256]{2,1,0:T(8,128)(2,1)S(1)}, bf16[2,528,256]{2,1,0:T(8,128)(2,1)}, u32[]{:S(2)}) %copy-start.1) | copy-done | bytes 540696
  2.5 0.0 copy-start.2
  2.5 1.0 %copy-done.2 = f32[256,512]{1,0:T(8,128)S(1)} copy-done((f32[256,512]{1,0:T(8,128)S(1)}, f32[256,512]{1,0:T(8,128)}, u32[]{:S(2)}) %copy-start.2) | copy-done | bytes 524312
  3.5 0.0 copy-start.3
  3.5 1.0 %copy-done.3 = bf16[3,256,256]{2,1,0:T(8,128)(2,1)S(1)} copy-done((bf16[3,256,256]{2,1,0:T(8,128)(2,1)S(1)}, bf16[3,256,256]{2,1,0:T(8,128)(2,1)}, u32[]{:S(2)}) %copy-start.3) | copy-done | bytes 393240
  4.5 45.0 %shard_map.46 = f32[128,1024]{1,0:T(8,128)S(1)} custom-call(f32[3,64,2048]{2,1,0:T(8,128)S(1)} %bitcast.1, bf16[2,528,256]{2,1,0:T(8,128)(2,1)S(1)} %copy-done.1, bf16[3,256,256]{2,1,0:T(8,128)(2,1)S(1)} %copy-done.3, f32[256,512]{1,0:T(8,128)S(1)} %copy-done.2), custom_call_target="tpu_custom_call" | custom-call | tf_op jit(solution)/shard_map/pallas_call | solution.py:364
  49.6 0.9 %broadcast_divide_fusion = f32[128,1024]{1,0:T(8,128)} fusion(f32[128,1024]{1,0:T(8,128)S(1)} %shard_map.46, f32[1024]{0:T(1024)S(1)} %subtract_convert_fusion), kind=kLoop, calls=%fused_computation | loop fusion | flops 131072 | bytes 1052672 | tf_op jit(solution)/shard_map/div | solution.py:393
  (1 shorter events, 0.0 us)
Async XLA Ops:
  0.0 1.4 %copy-start = (f32[64,3,2048]{2,0,1:T(8,128)S(1)}, f32[64,3,2048]{2,0,1:T(8,128)}, u32[]{:S(2)}) copy-start(f32[64,3,2048]{2,0,1:T(8,128)} %param.4) | copy-start | bytes 4718596
  1.4 1.0 %copy-start.1 = (bf16[2,528,256]{2,1,0:T(8,128)(2,1)S(1)}, bf16[2,528,256]{2,1,0:T(8,128)(2,1)}, u32[]{:S(2)}) copy-start(bf16[2,528,256]{2,1,0:T(8,128)(2,1)} %constant.8.clone.forward) | copy-start | bytes 1622020
  2.5 1.0 %copy-start.2 = (f32[256,512]{1,0:T(8,128)S(1)}, f32[256,512]{1,0:T(8,128)}, u32[]{:S(2)}) copy-start(f32[256,512]{1,0:T(8,128)} %constant.10.clone.inverse) | copy-start | bytes 1572868
  3.5 1.0 %copy-start.3 = (bf16[3,256,256]{2,1,0:T(8,128)(2,1)S(1)}, bf16[3,256,256]{2,1,0:T(8,128)(2,1)}, u32[]{:S(2)}) copy-start(bf16[3,256,256]{2,1,0:T(8,128)(2,1)} %constant.9.clone.sums) | copy-start | bytes 1179652

commit v2 on v1

--- a/solution.py
+++ b/solution.py
@@ -228,7 +228,6 @@
 
     lax.fori_loop(1, groups, tell_start, 0)
     send_component(1)
-    send_component(2)
     msgs[pl.ds(me, 1)] = total[...][None]
 
     acc_re[...] = jnp.zeros_like(acc_re)
@@ -261,6 +260,13 @@
         return carry
 
     lax.fori_loop(0, groups, spread, 0)
+
+    def sent(c):
+        gone = recv.at[c, pl.ds(0, (groups - 1) * frames), :]
+        pltpu.make_async_copy(gone, gone, send_sem.at[c]).wait()
+
+    sent(0)
+    send_component(2)
 
     def lanes_of(value):
         return [value[:, i * width : (i + 1) * width] for i in range(blocks)]
@@ -343,12 +349,8 @@
     for i, piece in enumerate(lanes_of(result)):
         out[:, i * BLOCK : (i + 1) * BLOCK] = jnp.transpose(piece)
 
-    def sent(c, carry):
-        gone = recv.at[c, pl.ds(0, (groups - 1) * frames), :]
-        pltpu.make_async_copy(gone, gone, send_sem.at[c]).wait()
-        return carry
-
-    lax.fori_loop(0, 3, sent, 0)
+    sent(1)
+    sent(2)
 
 
 def fused(displacements):
@@ -364,7 +366,7 @@
     numerator = pl.pallas_call(
         functools.partial(kernel, groups, atom_count * lax.axis_size("atoms")),
         out_shape=jax.ShapeDtypeStruct((width, length), f32),
-        in_specs=[pl.BlockSpec(memory_space=pl.ANY)] * 4,
+        in_specs=[pl.BlockSpec(memory_space=pltpu.HBM)] * 4,
         out_specs=pl.BlockSpec(memory_space=pltpu.VMEM),
         scratch_shapes=[
             pltpu.VMEM((3, frames, atom_count), f32),
@@ -386,7 +388,7 @@
             dma, dma, dma((groups,)), dma((groups,)),
         ],
         compiler_params=pltpu.CompilerParams(
-            collective_id=0, has_side_effects=True, vmem_limit_bytes=40 * 1024 * 1024
+            collective_id=0, has_side_effects=True, vmem_limit_bytes=60 * 1024 * 1024
         ),
     )(jnp.transpose(displacements, (1, 0, 2)), jnp.asarray(forward), jnp.asarray(sums), jnp.asarray(inverse))
     counts = (length - jnp.arange(length)).astype(f32)

time: 50.7 us -> 47.7 us (0.941)
  local copies, waits for them, and re-layouts: 4.49 us -> 0 us
  other arithmetic: 0.86 us -> 1.9 us
  Pallas kernels: 45 us -> 45.7 us
    unnamed x8 -> x0, local copies, waits for them, and re-layouts: 4.49 us -> none
    div x1, other arithmetic: 0.85 us -> 1.89 us  [fused(): return numerator / counts[None, :]]
    pallas_call x1, Pallas kernels: 45 us -> 45.7 us  [fused(): pl.pallas_call(functools.partial(kernel, groups, atom_count * lax.axis_si...]
where the time goes in v2:
time: 47.7 us; the launch traced here: 47.6 us
  Pallas kernels  45.7 us (96%)
  other arithmetic  1.9 us (4%)
    pallas_call x1, Pallas kernels, fused(): pl.pallas_call(functools.partial(kernel, groups, atom_count * lax.axis_si...  45.7 us
    div x1, other arithmetic, fused(): return numerator / counts[None, :]  1.89 us

profile of v2, /device:TPU:0, one launch (start us, length us, event | category | flops | bytes accessed | tf_op | source)
XLA Modules:
  0.0 47.6 jit_solution(6209991616616768465)
XLA Ops:
  0.0 45.7 %shard_map.46 = f32[128,1024]{1,0:T(8,128)} custom-call(f32[3,64,2048]{2,1,0:T(8,128)} %bitcast.1, bf16[2,528,256]{2,1,0:T(8,128)(2,1)} %constant.8.clone.forward, bf16[3,256,256]{2,1,0:T(8,128)(2,1)} %constant.9.clone.sums, f32[256,512]{1,0:T(8,128)} %constant.10.clone.inverse), custom_call_target="tpu_custom_call" | custom-call | tf_op jit(solution)/shard_map/pallas_call | solution.py:366
  45.7 1.9 %broadcast_divide_fusion = f32[128,1024]{1,0:T(8,128)} fusion(f32[128,1024]{1,0:T(8,128)} %shard_map.46, f32[1024]{0:T(1024)S(1)} %subtract_convert_fusion), kind=kLoop, calls=%fused_computation | loop fusion | flops 131072 | bytes 1052672 | tf_op jit(solution)/shard_map/div | solution.py:395
  (1 shorter events, 0.0 us)

commit v3 on v1

--- a/solution.py
+++ b/solution.py
@@ -168,26 +168,31 @@
     lax.fori_loop(1, groups, greet, 0)
     pl.semaphore_wait(barrier, groups)
 
-    def far_first(t):
-        return groups // 2 + (1 - 2 * lax.rem(t, 2)) * ((t + 1) // 2)
-
-    def send_component(c):
-        def send(t, carry):
-            peer = peer_at(far_first(t))
+    half = groups // 2
+    side = me // half
+    spot = lax.rem(me, half)
+
+    def send_half(c, far):
+        start = (1 - side if far else side) * half
+
+        def send(k, carry):
+            peer = start + lax.rem(spot + k, half)
             pltpu.make_async_remote_copy(
                 src_ref=x.at[c, :, pl.ds(pl.multiple_of(peer * width, width), width)],
                 dst_ref=recv.at[c, pl.ds(pl.multiple_of(me * frames, frames), frames), :],
-                send_sem=send_sem.at[c],
-                recv_sem=recv_sem.at[c],
+                send_sem=send_sem.at[c, int(far)],
+                recv_sem=recv_sem.at[c, int(far)],
                 device_id={"frames": peer},
                 device_id_type=MESH,
             ).start()
             return carry
 
-        lax.fori_loop(0, groups - 1, send, 0)
-        own_copy(c).start()
-
-    send_component(0)
+        lax.fori_loop(0 if far else 1, half, send, 0)
+        if not far:
+            own_copy(c).start()
+
+    send_half(0, True)
+    send_half(0, False)
 
     parts = []
     for c in range(3):
@@ -227,8 +232,9 @@
         return carry
 
     lax.fori_loop(1, groups, tell_start, 0)
-    send_component(1)
-    send_component(2)
+    send_half(1, True)
+    send_half(1, False)
+    send_half(2, False)
     msgs[pl.ds(me, 1)] = total[...][None]
 
     acc_re[...] = jnp.zeros_like(acc_re)
@@ -262,34 +268,53 @@
 
     lax.fori_loop(0, groups, spread, 0)
 
+    def several(c, far):
+        return recv.at[c, pl.ds(0, (half if far else half - 1) * frames), :]
+
+    def sent(c, far):
+        gone = several(c, far)
+        pltpu.make_async_copy(gone, gone, send_sem.at[c, int(far)]).wait()
+
+    def arrived(c, far):
+        came = several(c, far)
+        pltpu.make_async_copy(came, came, recv_sem.at[c, int(far)]).wait()
+
+    sent(0, True)
+    send_half(2, True)
+
     def lanes_of(value):
-        return [value[:, i * width : (i + 1) * width] for i in range(blocks)]
+        return [value[:, i : i + width] for i in range(0, value.shape[1], width)]
+
+    def transform(c, which):
+        pieces = []
+        for i in range(blocks // 2):
+            at = pl.ds(pl.multiple_of((which * (blocks // 2) + i) * BLOCK, BLOCK), BLOCK)
+            pieces.append(recv[c, at, :] - drift[c, at, :])
+        high, mid, low = split(jnp.concatenate(pieces, axis=1), 3)
+        running = mm(sv[0], high) + (mm(sv[0], mid) + mm(sv[0], low))
+        first, second = lanes_of(running[BLOCK - 1 : BLOCK, :])
+        later = jnp.full((1, 1), which, jnp.int32).astype(jnp.float32)
+        sooner = 1.0 - later
+        shift = jnp.concatenate([-sooner * (first + second), later * first - sooner * second], axis=1)
+        positions = running + shift
+        squares[which] += positions * positions
+        high, low = split(positions, 2)
+        spectrum[which] = mm(fv[0], high) + (mm(fv[0], low) + mm(fv[1], high))
+
+    def spectra(at):
+        return lanes_of(spectrum[0, at, :]) + lanes_of(spectrum[1, at, :])
 
     def component(c, carry):
-        arrived = recv.at[c, pl.ds(0, (groups - 1) * frames), :]
         own_copy(c).wait()
-        pltpu.make_async_copy(arrived, arrived, recv_sem.at[c]).wait()
-        centred = jnp.concatenate(
-            [
-                recv[c, i * BLOCK : (i + 1) * BLOCK, :] - drift[c, i * BLOCK : (i + 1) * BLOCK, :]
-                for i in range(blocks)
-            ],
-            axis=1,
-        )
-        high, mid, low = split(centred, 3)
-        running = mm(sv[0], high) + (mm(sv[0], mid) + mm(sv[0], low))
-        before = [jnp.zeros((1, width), jnp.float32)]
-        for last in lanes_of(running[BLOCK - 1 : BLOCK, :])[:-1]:
-            before.append(before[-1] + last)
-        positions = running + jnp.concatenate(before, axis=1)
-        squares[...] += positions * positions
-        high, low = split(positions, 2)
-        spectrum[...] = mm(fv[0], high) + (mm(fv[0], low) + mm(fv[1], high))
+        arrived(c, False)
+        transform(c, side)
+        arrived(c, True)
+        transform(c, 1 - side)
 
         def rows(r, inner):
             at = pl.ds(pl.multiple_of(r * 8, 8), 8)
-            re = lanes_of(spectrum[at, :])
-            im = lanes_of(spectrum[pl.ds(pl.multiple_of(BLOCK + r * 8, 8), 8), :])
+            re = spectra(at)
+            im = spectra(pl.ds(pl.multiple_of(BLOCK + r * 8, 8), 8))
             for d in range(blocks):
                 here = slice(d * width, (d + 1) * width)
                 real = acc_re[at, here]
@@ -305,7 +330,7 @@
             return inner
 
         lax.fori_loop(0, BLOCK // 8, rows, 0, unroll=2)
-        top = lanes_of(spectrum[2 * BLOCK : 2 * BLOCK + 8, :])
+        top = spectra(pl.ds(2 * BLOCK, 8))
         for d in range(blocks):
             here = slice(d * width, (d + 1) * width)
             value = acc_top[:, here]
@@ -328,7 +353,7 @@
         iv[...], cross, precision=lax.Precision.HIGHEST, preferred_element_type=jnp.float32
     )
     corr = corr - (top + next_block(top)) * (parity * (1.0 / BLOCK))
-    parts = split(squares[...], 3)
+    parts = split(jnp.concatenate([squares[0], squares[1]], axis=1), 3)
     later = mm(sv[1], parts[0]) + (mm(sv[1], parts[1]) + mm(sv[1], parts[2]))
     parts = [jnp.concatenate(lanes_of(part)[::-1], axis=1) for part in parts]
     earlier = mm(sv[2], parts[0]) + (mm(sv[2], parts[1]) + mm(sv[2], parts[2]))
@@ -343,12 +368,8 @@
     for i, piece in enumerate(lanes_of(result)):
         out[:, i * BLOCK : (i + 1) * BLOCK] = jnp.transpose(piece)
 
-    def sent(c, carry):
-        gone = recv.at[c, pl.ds(0, (groups - 1) * frames), :]
-        pltpu.make_async_copy(gone, gone, send_sem.at[c]).wait()
-        return carry
-
-    lax.fori_loop(0, 3, sent, 0)
+    for c, far in ((0, False), (1, True), (1, False), (2, False), (2, True)):
+        sent(c, far)
 
 
 def fused(displacements):
@@ -364,7 +385,7 @@
     numerator = pl.pallas_call(
         functools.partial(kernel, groups, atom_count * lax.axis_size("atoms")),
         out_shape=jax.ShapeDtypeStruct((width, length), f32),
-        in_specs=[pl.BlockSpec(memory_space=pl.ANY)] * 4,
+        in_specs=[pl.BlockSpec(memory_space=pltpu.HBM)] * 4,
         out_specs=pl.BlockSpec(memory_space=pltpu.VMEM),
         scratch_shapes=[
             pltpu.VMEM((3, frames, atom_count), f32),
@@ -377,12 +398,12 @@
             pltpu.VMEM(sums.shape, bf16),
             pltpu.VMEM(inverse.shape, f32),
             pltpu.VMEM((3, length, width), f32),
-            pltpu.VMEM((2 * BLOCK + 16, blocks * width), f32),
+            pltpu.VMEM((2, 2 * BLOCK + 16, blocks * width // 2), f32),
             pltpu.VMEM((BLOCK, blocks * width), f32),
             pltpu.VMEM((BLOCK, blocks * width), f32),
             pltpu.VMEM((8, blocks * width), f32),
-            pltpu.VMEM((BLOCK, blocks * width), f32),
-            dma((3,)), dma((3,)), dma((3,)), dma((3,)), dma((3,)),
+            pltpu.VMEM((2, BLOCK, blocks * width // 2), f32),
+            dma((3,)), dma((3,)), dma((3,)), dma((3, 2)), dma((3, 2)),
             dma, dma, dma((groups,)), dma((groups,)),
         ],
         compiler_params=pltpu.CompilerParams(
@@ -396,8 +417,9 @@
 def fits(mesh, shape):
     groups, pairs = mesh.shape["frames"], mesh.shape["atoms"]
     length, _, atoms = shape
-    frames = length // groups
-    return pairs == 2 and atoms // (pairs * groups) == LANES and frames % 8 == 0 and length % BLOCK == 0
+    if pairs != 2 or groups % 2 or atoms != pairs * groups * LANES or length != 4 * BLOCK:
+        return False
+    return length // groups % 8 == 0
 
 
 def solution(mesh):

time: 50.7 us -> 51.5 us (1.016)
  Pallas kernels: 45 us -> 45.8 us
    pallas_call x1, Pallas kernels: 45 us -> 45.8 us  [fused(): pl.pallas_call(functools.partial(kernel, groups, atom_count * lax.axis_si...]
where the time goes in v3:
time: 51.5 us; the launch traced here: 51.2 us
  Pallas kernels  45.8 us (89%)
  local copies, waits for them, and re-layouts  4.49 us (9%)
  other arithmetic  0.86 us (2%)
    pallas_call x1, Pallas kernels, fused(): pl.pallas_call(functools.partial(kernel, groups, atom_count * lax.axis_si...  45.8 us
    unnamed x8, local copies, waits for them, and re-layouts  4.49 us

profile of v3, /device:TPU:0, one launch (start us, length us, event | category | flops | bytes accessed | tf_op | source)
XLA Modules:
  0.0 51.2 jit_solution(8144257199275107739)
XLA Ops:
  0.0 0.0 copy-start
  0.0 1.4 %copy-done = f32[64,3,2048]{2,0,1:T(8,128)S(1)} copy-done((f32[64,3,2048]{2,0,1:T(8,128)S(1)}, f32[64,3,2048]{2,0,1:T(8,128)}, u32[]{:S(2)}) %copy-start) | copy-done | bytes 1572888
  1.4 0.0 copy-start.1
  1.4 1.0 %copy-done.1 = bf16[2,528,256]{2,1,0:T(8,128)(2,1)S(1)} copy-done((bf16[2,528,256]{2,1,0:T(8,128)(2,1)S(1)}, bf16[2,528,256]{2,1,0:T(8,128)(2,1)}, u32[]{:S(2)}) %copy-start.1) | copy-done | bytes 540696
  2.5 0.0 copy-start.2
  2.5 1.0 %copy-done.2 = f32[256,512]{1,0:T(8,128)S(1)} copy-done((f32[256,512]{1,0:T(8,128)S(1)}, f32[256,512]{1,0:T(8,128)}, u32[]{:S(2)}) %copy-start.2) | copy-done | bytes 524312
  3.5 0.0 copy-start.3
  3.5 1.0 %copy-done.3 = bf16[3,256,256]{2,1,0:T(8,128)(2,1)S(1)} copy-done((bf16[3,256,256]{2,1,0:T(8,128)(2,1)S(1)}, bf16[3,256,256]{2,1,0:T(8,128)(2,1)}, u32[]{:S(2)}) %copy-start.3) | copy-done | bytes 393240
  4.5 45.8 %shard_map.46 = f32[128,1024]{1,0:T(8,128)S(1)} custom-call(f32[3,64,2048]{2,1,0:T(8,128)S(1)} %bitcast.1, bf16[2,528,256]{2,1,0:T(8,128)(2,1)S(1)} %copy-done.1, bf16[3,256,256]{2,1,0:T(8,128)(2,1)S(1)} %copy-done.3, f32[256,512]{1,0:T(8,128)S(1)} %copy-done.2), custom_call_target="tpu_custom_call" | custom-call | tf_op jit(solution)/shard_map/pallas_call | solution.py:385
  50.4 0.9 %broadcast_divide_fusion = f32[128,1024]{1,0:T(8,128)} fusion(f32[128,1024]{1,0:T(8,128)S(1)} %shard_map.46, f32[1024]{0:T(1024)S(1)} %subtract_convert_fusion), kind=kLoop, calls=%fused_computation | loop fusion | flops 131072 | bytes 1052672 | tf_op jit(solution)/shard_map/div | solution.py:414
  (1 shorter events, 0.0 us)
Async XLA Ops:
  0.0 1.4 %copy-start = (f32[64,3,2048]{2,0,1:T(8,128)S(1)}, f32[64,3,2048]{2,0,1:T(8,128)}, u32[]{:S(2)}) copy-start(f32[64,3,2048]{2,0,1:T(8,128)} %param.4) | copy-start | bytes 4718596
  1.4 1.0 %copy-start.1 = (bf16[2,528,256]{2,1,0:T(8,128)(2,1)S(1)}, bf16[2,528,256]{2,1,0:T(8,128)(2,1)}, u32[]{:S(2)}) copy-start(bf16[2,528,256]{2,1,0:T(8,128)(2,1)} %constant.8.clone.forward) | copy-start | bytes 1622020
  2.5 1.0 %copy-start.2 = (f32[256,512]{1,0:T(8,128)S(1)}, f32[256,512]{1,0:T(8,128)}, u32[]{:S(2)}) copy-start(f32[256,512]{1,0:T(8,128)} %constant.10.clone.inverse) | copy-start | bytes 1572868
  3.5 1.0 %copy-start.3 = (bf16[3,256,256]{2,1,0:T(8,128)(2,1)S(1)}, bf16[3,256,256]{2,1,0:T(8,128)(2,1)}, u32[]{:S(2)}) copy-start(bf16[3,256,256]{2,1,0:T(8,128)(2,1)} %constant.9.clone.sums) | copy-start | bytes 1179652

commit v4 on v3

--- a/solution.py
+++ b/solution.py
@@ -101,17 +101,23 @@
     forward[:BLOCK] = np.cos(angle)
     forward[BLOCK:points] = -np.sin(angle)
     forward[points] = 1.0 - 2.0 * (index % 2)
-    high = forward.astype(ml_dtypes.bfloat16)
-    low = (forward - high.astype(np.float64)).astype(ml_dtypes.bfloat16)
     weight = np.where(index == 0, 1.0, 2.0)[None, :] / points
-    inverse = np.concatenate([np.cos(angle) * weight, -np.sin(angle) * weight], axis=1)
+    inverse = [-2.0 * np.cos(angle) * weight, 2.0 * np.sin(angle) * weight]
     row, col = index[:, None], index[None, :]
-    sums = np.stack([col <= row, col >= row, col <= BLOCK - 1 - row])
-    return (
-        np.stack([high, low]),
-        sums.astype(ml_dtypes.bfloat16),
-        (-2.0 * inverse).astype(np.float32),
-    )
+    sums = [col <= row, col >= row, col <= BLOCK - 1 - row]
+    pieces = rounded(forward, 2)
+    pieces += [part.astype(ml_dtypes.bfloat16) for part in sums]
+    pieces += [part for pair in zip(*(rounded(half, 3) for half in inverse)) for part in pair]
+    return np.concatenate(pieces, axis=0)
+
+
+def rounded(values, terms):
+    parts = []
+    for _ in range(terms):
+        part = values.astype(ml_dtypes.bfloat16)
+        parts.append(part)
+        values = values - part.astype(np.float64)
+    return parts
 
 
 def split(value, terms):
@@ -128,8 +134,8 @@
 
 
 def kernel(
-    groups, atom_total, x, forward, sums, inverse, out,
-    xv, recv, mine, sibling, total, msgs, fv, sv, iv, drift, spectrum, acc_re, acc_im, acc_top, squares,
+    groups, atom_total, x, table, out,
+    xv, recv, mine, sibling, total, msgs, held, drift, spectrum, acc_re, acc_im, acc_top, squares,
     load_sem, const_sem, own_sem, send_sem, recv_sem, pair_send, pair_recv, msg_send, msg_recv,
 ):
     me, core = lax.axis_index("frames"), lax.axis_index("atoms")
@@ -141,12 +147,20 @@
     loads = [pltpu.make_async_copy(x.at[c], xv.at[c], load_sem.at[c]) for c in range(3)]
     for load in loads:
         load.start()
-    consts = [
-        pltpu.make_async_copy(src, dst, const_sem.at[i])
-        for i, (src, dst) in enumerate(((forward, fv), (sums, sv), (inverse, iv)))
-    ]
-    for const in consts:
-        const.start()
+    const = pltpu.make_async_copy(table, held, const_sem)
+    const.start()
+    tall = 2 * BLOCK + 16
+
+    def forward(part):
+        return held[part * tall : (part + 1) * tall, :]
+
+    def sums(which):
+        start = 2 * tall + which * BLOCK
+        return held[start : start + BLOCK, :]
+
+    def inverse(part, which):
+        start = 2 * tall + (3 + 2 * part + which) * BLOCK
+        return held[start : start + BLOCK, :]
 
     def peer_at(k):
         return lax.rem(me + k, groups)
@@ -172,27 +186,28 @@
     side = me // half
     spot = lax.rem(me, half)
 
-    def send_half(c, far):
-        start = (1 - side if far else side) * half
-
+    def send_one(c, far, k):
+        peer = (1 - side if far else side) * half + lax.rem(spot + k, half)
+        pltpu.make_async_remote_copy(
+            src_ref=x.at[c, :, pl.ds(pl.multiple_of(peer * width, width), width)],
+            dst_ref=recv.at[c, pl.ds(pl.multiple_of(me * frames, frames), frames), :],
+            send_sem=send_sem.at[c, int(far)],
+            recv_sem=recv_sem.at[c, int(far)],
+            device_id={"frames": peer},
+            device_id_type=MESH,
+        ).start()
+
+    def send_component(c):
         def send(k, carry):
-            peer = start + lax.rem(spot + k, half)
-            pltpu.make_async_remote_copy(
-                src_ref=x.at[c, :, pl.ds(pl.multiple_of(peer * width, width), width)],
-                dst_ref=recv.at[c, pl.ds(pl.multiple_of(me * frames, frames), frames), :],
-                send_sem=send_sem.at[c, int(far)],
-                recv_sem=recv_sem.at[c, int(far)],
-                device_id={"frames": peer},
-                device_id_type=MESH,
-            ).start()
+            send_one(c, True, k)
+            send_one(c, False, k)
             return carry
 
-        lax.fori_loop(0 if far else 1, half, send, 0)
-        if not far:
-            own_copy(c).start()
-
-    send_half(0, True)
-    send_half(0, False)
+        send_one(c, True, 0)
+        lax.fori_loop(1, half, send, 0)
+        own_copy(c).start()
+
+    send_component(0)
 
     parts = []
     for c in range(3):
@@ -232,17 +247,14 @@
         return carry
 
     lax.fori_loop(1, groups, tell_start, 0)
-    send_half(1, True)
-    send_half(1, False)
-    send_half(2, False)
+    send_component(1)
     msgs[pl.ds(me, 1)] = total[...][None]
 
     acc_re[...] = jnp.zeros_like(acc_re)
     acc_im[...] = jnp.zeros_like(acc_im)
     acc_top[...] = jnp.zeros_like(acc_top)
     squares[...] = jnp.zeros_like(squares)
-    for const in consts:
-        const.wait()
+    const.wait()
 
     def heard(k, carry):
         source = lax.rem(me + groups - k, groups)
@@ -280,7 +292,7 @@
         pltpu.make_async_copy(came, came, recv_sem.at[c, int(far)]).wait()
 
     sent(0, True)
-    send_half(2, True)
+    send_component(2)
 
     def lanes_of(value):
         return [value[:, i : i + width] for i in range(0, value.shape[1], width)]
@@ -291,7 +303,7 @@
             at = pl.ds(pl.multiple_of((which * (blocks // 2) + i) * BLOCK, BLOCK), BLOCK)
             pieces.append(recv[c, at, :] - drift[c, at, :])
         high, mid, low = split(jnp.concatenate(pieces, axis=1), 3)
-        running = mm(sv[0], high) + (mm(sv[0], mid) + mm(sv[0], low))
+        running = mm(sums(0), high) + (mm(sums(0), mid) + mm(sums(0), low))
         first, second = lanes_of(running[BLOCK - 1 : BLOCK, :])
         later = jnp.full((1, 1), which, jnp.int32).astype(jnp.float32)
         sooner = 1.0 - later
@@ -299,7 +311,7 @@
         positions = running + shift
         squares[which] += positions * positions
         high, low = split(positions, 2)
-        spectrum[which] = mm(fv[0], high) + (mm(fv[0], low) + mm(fv[1], high))
+        spectrum[which] = mm(forward(0), high) + (mm(forward(0), low) + mm(forward(1), high))
 
     def spectra(at):
         return lanes_of(spectrum[0, at, :]) + lanes_of(spectrum[1, at, :])
@@ -346,17 +358,15 @@
 
     parity = (1 - 2 * (lax.broadcasted_iota(jnp.int32, (BLOCK, 1), 0) % 2)).astype(jnp.float32)
     real, imag, top = acc_re[...], acc_im[...], acc_top[0:1, :]
-    cross = jnp.concatenate(
-        [real + parity * next_block(real), imag + parity * next_block(imag)], axis=0
-    )
-    corr = jnp.dot(
-        iv[...], cross, precision=lax.Precision.HIGHEST, preferred_element_type=jnp.float32
-    )
+    cross = [split(real + parity * next_block(real), 3), split(imag + parity * next_block(imag), 3)]
+    corr = jnp.zeros_like(real)
+    for a, b in ((2, 0), (0, 2), (1, 1), (1, 0), (0, 1), (0, 0)):
+        corr = corr + (mm(inverse(a, 0), cross[0][b]) + mm(inverse(a, 1), cross[1][b]))
     corr = corr - (top + next_block(top)) * (parity * (1.0 / BLOCK))
     parts = split(jnp.concatenate([squares[0], squares[1]], axis=1), 3)
-    later = mm(sv[1], parts[0]) + (mm(sv[1], parts[1]) + mm(sv[1], parts[2]))
+    later = mm(sums(1), parts[0]) + (mm(sums(1), parts[1]) + mm(sums(1), parts[2]))
     parts = [jnp.concatenate(lanes_of(part)[::-1], axis=1) for part in parts]
-    earlier = mm(sv[2], parts[0]) + (mm(sv[2], parts[1]) + mm(sv[2], parts[2]))
+    earlier = mm(sums(2), parts[0]) + (mm(sums(2), parts[1]) + mm(sums(2), parts[2]))
     sums_of = lanes_of(later[0:1, :])
     whole = []
     for i in range(blocks):
@@ -378,14 +388,14 @@
     length = frames * groups
     width = atom_count // groups
     blocks = length // BLOCK
-    forward, sums, inverse = tables()
+    table = tables()
     lanes = -(-3 * frames // LANES) * LANES
     f32, bf16 = jnp.float32, jnp.bfloat16
     dma = pltpu.SemaphoreType.DMA
     numerator = pl.pallas_call(
         functools.partial(kernel, groups, atom_count * lax.axis_size("atoms")),
         out_shape=jax.ShapeDtypeStruct((width, length), f32),
-        in_specs=[pl.BlockSpec(memory_space=pltpu.HBM)] * 4,
+        in_specs=[pl.BlockSpec(memory_space=pltpu.HBM)] * 2,
         out_specs=pl.BlockSpec(memory_space=pltpu.VMEM),
         scratch_shapes=[
             pltpu.VMEM((3, frames, atom_count), f32),
@@ -394,22 +404,20 @@
             pltpu.VMEM((1, lanes), f32),
             pltpu.VMEM((1, lanes), f32),
             pltpu.VMEM((groups, 1, lanes), f32),
-            pltpu.VMEM(forward.shape, bf16),
-            pltpu.VMEM(sums.shape, bf16),
-            pltpu.VMEM(inverse.shape, f32),
+            pltpu.VMEM(table.shape, bf16),
             pltpu.VMEM((3, length, width), f32),
             pltpu.VMEM((2, 2 * BLOCK + 16, blocks * width // 2), f32),
             pltpu.VMEM((BLOCK, blocks * width), f32),
             pltpu.VMEM((BLOCK, blocks * width), f32),
             pltpu.VMEM((8, blocks * width), f32),
             pltpu.VMEM((2, BLOCK, blocks * width // 2), f32),
-            dma((3,)), dma((3,)), dma((3,)), dma((3, 2)), dma((3, 2)),
+            dma((3,)), dma, dma((3,)), dma((3, 2)), dma((3, 2)),
             dma, dma, dma((groups,)), dma((groups,)),
         ],
         compiler_params=pltpu.CompilerParams(
-            collective_id=0, has_side_effects=True, vmem_limit_bytes=40 * 1024 * 1024
+            collective_id=0, has_side_effects=True, vmem_limit_bytes=62_200_000
         ),
-    )(jnp.transpose(displacements, (1, 0, 2)), jnp.asarray(forward), jnp.asarray(sums), jnp.asarray(inverse))
+    )(jnp.transpose(displacements, (1, 0, 2)), jnp.asarray(table))
     counts = (length - jnp.arange(length)).astype(f32)
     return numerator / counts[None, :]
 

time: 51.5 us -> 48.4 us (0.940)
  local copies, waits for them, and re-layouts: 4.49 us -> 0 us
  other arithmetic: 0.86 us -> 1.9 us
  Pallas kernels: 45.8 us -> 46.4 us
    unnamed x8 -> x0, local copies, waits for them, and re-layouts: 4.49 us -> none
    div x1, other arithmetic: 0.85 us -> 1.89 us  [fused(): return numerator / counts[None, :]]
    pallas_call x1, Pallas kernels: 45.8 us -> 46.4 us  [fused(): pl.pallas_call(functools.partial(kernel, groups, atom_count * lax.axis_si...]
where the time goes in v4:
time: 48.4 us; the launch traced here: 48.3 us
  Pallas kernels  46.4 us (96%)
  other arithmetic  1.9 us (4%)
    pallas_call x1, Pallas kernels, fused(): pl.pallas_call(functools.partial(kernel, groups, atom_count * lax.axis_si...  46.4 us
    div x1, other arithmetic, fused(): return numerator / counts[None, :]  1.89 us

profile of v4, /device:TPU:0, one launch (start us, length us, event | category | flops | bytes accessed | tf_op | source)
XLA Modules:
  0.0 48.3 jit_solution(2622894701496368678)
XLA Ops:
  0.0 46.4 %shard_map.28 = f32[128,1024]{1,0:T(8,128)} custom-call(f32[3,64,2048]{2,1,0:T(8,128)} %bitcast.1, bf16[3360,256]{1,0:T(8,128)(2,1)} %constant.4.clone.table), custom_call_target="tpu_custom_call" | custom-call | tf_op jit(solution)/shard_map/pallas_call | solution.py:395
  46.4 1.9 %broadcast_divide_fusion = f32[128,1024]{1,0:T(8,128)} fusion(f32[128,1024]{1,0:T(8,128)} %shard_map.28, f32[1024]{0:T(1024)S(1)} %subtract_convert_fusion), kind=kLoop, calls=%fused_computation | loop fusion | flops 131072 | bytes 1052672 | tf_op jit(solution)/shard_map/div | solution.py:422
  (1 shorter events, 0.0 us)

commit v5 on v4

--- a/solution.py
+++ b/solution.py
@@ -107,7 +107,7 @@
     sums = [col <= row, col >= row, col <= BLOCK - 1 - row]
     pieces = rounded(forward, 2)
     pieces += [part.astype(ml_dtypes.bfloat16) for part in sums]
-    pieces += [part for pair in zip(*(rounded(half, 3) for half in inverse)) for part in pair]
+    pieces += [part for pair in zip(*(rounded(half, 2) for half in inverse)) for part in pair]
     return np.concatenate(pieces, axis=0)
 
 
@@ -302,8 +302,8 @@
         for i in range(blocks // 2):
             at = pl.ds(pl.multiple_of((which * (blocks // 2) + i) * BLOCK, BLOCK), BLOCK)
             pieces.append(recv[c, at, :] - drift[c, at, :])
-        high, mid, low = split(jnp.concatenate(pieces, axis=1), 3)
-        running = mm(sums(0), high) + (mm(sums(0), mid) + mm(sums(0), low))
+        high, low = split(jnp.concatenate(pieces, axis=1), 2)
+        running = mm(sums(0), high) + mm(sums(0), low)
         first, second = lanes_of(running[BLOCK - 1 : BLOCK, :])
         later = jnp.full((1, 1), which, jnp.int32).astype(jnp.float32)
         sooner = 1.0 - later
@@ -341,7 +341,7 @@
                     acc_im[at, here] = imag
             return inner
 
-        lax.fori_loop(0, BLOCK // 8, rows, 0, unroll=2)
+        lax.fori_loop(0, BLOCK // 8, rows, 0, unroll=4)
         top = spectra(pl.ds(2 * BLOCK, 8))
         for d in range(blocks):
             here = slice(d * width, (d + 1) * width)
@@ -358,15 +358,15 @@
 
     parity = (1 - 2 * (lax.broadcasted_iota(jnp.int32, (BLOCK, 1), 0) % 2)).astype(jnp.float32)
     real, imag, top = acc_re[...], acc_im[...], acc_top[0:1, :]
-    cross = [split(real + parity * next_block(real), 3), split(imag + parity * next_block(imag), 3)]
+    cross = [split(real + parity * next_block(real), 2), split(imag + parity * next_block(imag), 2)]
     corr = jnp.zeros_like(real)
-    for a, b in ((2, 0), (0, 2), (1, 1), (1, 0), (0, 1), (0, 0)):
+    for a, b in ((1, 0), (0, 1), (0, 0)):
         corr = corr + (mm(inverse(a, 0), cross[0][b]) + mm(inverse(a, 1), cross[1][b]))
     corr = corr - (top + next_block(top)) * (parity * (1.0 / BLOCK))
-    parts = split(jnp.concatenate([squares[0], squares[1]], axis=1), 3)
-    later = mm(sums(1), parts[0]) + (mm(sums(1), parts[1]) + mm(sums(1), parts[2]))
+    parts = split(jnp.concatenate([squares[0], squares[1]], axis=1), 2)
+    later = mm(sums(1), parts[0]) + mm(sums(1), parts[1])
     parts = [jnp.concatenate(lanes_of(part)[::-1], axis=1) for part in parts]
-    earlier = mm(sums(2), parts[0]) + (mm(sums(2), parts[1]) + mm(sums(2), parts[2]))
+    earlier = mm(sums(2), parts[0]) + mm(sums(2), parts[1])
     sums_of = lanes_of(later[0:1, :])
     whole = []
     for i in range(blocks):
@@ -376,7 +376,9 @@
         whole.append(value)
     result = later + earlier + jnp.concatenate(whole, axis=1) + corr
     for i, piece in enumerate(lanes_of(result)):
-        out[:, i * BLOCK : (i + 1) * BLOCK] = jnp.transpose(piece)
+        lag = i * BLOCK + lax.broadcasted_iota(jnp.int32, (BLOCK, 1), 0)
+        pairs = (blocks * BLOCK - lag).astype(jnp.float32)
+        out[:, i * BLOCK : (i + 1) * BLOCK] = jnp.transpose(piece / pairs)
 
     for c, far in ((0, False), (1, True), (1, False), (2, False), (2, True)):
         sent(c, far)
@@ -392,7 +394,7 @@
     lanes = -(-3 * frames // LANES) * LANES
     f32, bf16 = jnp.float32, jnp.bfloat16
     dma = pltpu.SemaphoreType.DMA
-    numerator = pl.pallas_call(
+    return pl.pallas_call(
         functools.partial(kernel, groups, atom_count * lax.axis_size("atoms")),
         out_shape=jax.ShapeDtypeStruct((width, length), f32),
         in_specs=[pl.BlockSpec(memory_space=pltpu.HBM)] * 2,
@@ -415,11 +417,9 @@
             dma, dma, dma((groups,)), dma((groups,)),
         ],
         compiler_params=pltpu.CompilerParams(
-            collective_id=0, has_side_effects=True, vmem_limit_bytes=62_200_000
+            collective_id=0, has_side_effects=True, vmem_limit_bytes=60 * 1024 * 1024
         ),
     )(jnp.transpose(displacements, (1, 0, 2)), jnp.asarray(table))
-    counts = (length - jnp.arange(length)).astype(f32)
-    return numerator / counts[None, :]
 
 
 def fits(mesh, shape):

time: 48.4 us -> 47.8 us (0.988)
  other arithmetic: 1.9 us -> 0 us
  local copies, waits for them, and re-layouts: 0 us -> 1.89 us
  Pallas kernels: 46.4 us -> 45.7 us
    div x1 -> x0, other arithmetic: 1.89 us -> none  [fused(): return numerator / counts[None, :]]
    unnamed x0 -> x1, local copies, waits for them, and re-layouts: none -> 1.89 us
    pallas_call x1, Pallas kernels: 46.4 us -> 45.7 us  [fused(): pl.pallas_call(functools.partial(kernel, groups, atom_count * lax.axis_si...]
where the time goes in v5:
time: 47.8 us; the launch traced here: 47.6 us
  Pallas kernels  45.7 us (96%)
  local copies, waits for them, and re-layouts  1.89 us (4%)
    pallas_call x1, Pallas kernels, fused(): pl.pallas_call(functools.partial(kernel, groups, atom_count * lax.axis_si...  45.7 us
    unnamed x1, local copies, waits for them, and re-layouts  1.89 us

profile of v5, /device:TPU:0, one launch (start us, length us, event | category | flops | bytes accessed | tf_op | source)
XLA Modules:
  0.0 47.6 jit_solution(10092706535032645256)
XLA Ops:
  0.0 45.7 %shard_map.28 = f32[128,1024]{1,0:T(8,128)} custom-call(f32[3,64,2048]{2,1,0:T(8,128)} %bitcast.1, bf16[2848,256]{1,0:T(8,128)(2,1)} %constant.2.clone.table), custom_call_target="tpu_custom_call" | custom-call | tf_op jit(solution)/shard_map/pallas_call | solution.py:397
  45.7 1.9 %copy.4 = f32[128,1024]{1,0:T(8,128)} copy(f32[128,1024]{1,0:T(8,128)} %shard_map.28) | data formatting | bytes 1048576

commit v6 on v5

--- a/solution.py
+++ b/solution.py
@@ -13,6 +13,7 @@
 
 BLOCK = 256
 LANES = 128
+PIECES = 8
 MESH = pl.DeviceIdType.MESH
 
 
@@ -186,25 +187,22 @@
     side = me // half
     spot = lax.rem(me, half)
 
-    def send_one(c, far, k):
-        peer = (1 - side if far else side) * half + lax.rem(spot + k, half)
-        pltpu.make_async_remote_copy(
-            src_ref=x.at[c, :, pl.ds(pl.multiple_of(peer * width, width), width)],
-            dst_ref=recv.at[c, pl.ds(pl.multiple_of(me * frames, frames), frames), :],
-            send_sem=send_sem.at[c, int(far)],
-            recv_sem=recv_sem.at[c, int(far)],
-            device_id={"frames": peer},
-            device_id_type=MESH,
-        ).start()
-
     def send_component(c):
-        def send(k, carry):
-            send_one(c, True, k)
-            send_one(c, False, k)
+        def send(t, carry):
+            offset = half + (1 - 2 * lax.rem(t, 2)) * ((t + 1) // 2)
+            peer = peer_at(offset)
+            far = lax.rem(peer // half + side, 2)
+            pltpu.make_async_remote_copy(
+                src_ref=x.at[c, :, pl.ds(pl.multiple_of(peer * width, width), width)],
+                dst_ref=recv.at[c, pl.ds(pl.multiple_of(me * frames, frames), frames), :],
+                send_sem=send_sem.at[c, far],
+                recv_sem=recv_sem.at[c, far],
+                device_id={"frames": peer},
+                device_id_type=MESH,
+            ).start()
             return carry
 
-        send_one(c, True, 0)
-        lax.fori_loop(1, half, send, 0)
+        lax.fori_loop(0, groups - 1, send, 0)
         own_copy(c).start()
 
     send_component(0)
@@ -248,6 +246,7 @@
 
     lax.fori_loop(1, groups, tell_start, 0)
     send_component(1)
+    send_component(2)
     msgs[pl.ds(me, 1)] = total[...][None]
 
     acc_re[...] = jnp.zeros_like(acc_re)
@@ -290,9 +289,6 @@
     def arrived(c, far):
         came = several(c, far)
         pltpu.make_async_copy(came, came, recv_sem.at[c, int(far)]).wait()
-
-    sent(0, True)
-    send_component(2)
 
     def lanes_of(value):
         return [value[:, i : i + width] for i in range(0, value.shape[1], width)]
@@ -380,8 +376,9 @@
         pairs = (blocks * BLOCK - lag).astype(jnp.float32)
         out[:, i * BLOCK : (i + 1) * BLOCK] = jnp.transpose(piece / pairs)
 
-    for c, far in ((0, False), (1, True), (1, False), (2, False), (2, True)):
-        sent(c, far)
+    for c in range(3):
+        sent(c, False)
+        sent(c, True)
 
 
 def fused(displacements):
@@ -394,7 +391,7 @@
     lanes = -(-3 * frames // LANES) * LANES
     f32, bf16 = jnp.float32, jnp.bfloat16
     dma = pltpu.SemaphoreType.DMA
-    return pl.pallas_call(
+    result = pl.pallas_call(
         functools.partial(kernel, groups, atom_count * lax.axis_size("atoms")),
         out_shape=jax.ShapeDtypeStruct((width, length), f32),
         in_specs=[pl.BlockSpec(memory_space=pltpu.HBM)] * 2,
@@ -420,6 +417,27 @@
             collective_id=0, has_side_effects=True, vmem_limit_bytes=60 * 1024 * 1024
         ),
     )(jnp.transpose(displacements, (1, 0, 2)), jnp.asarray(table))
+    return pl.pallas_call(
+        deliver,
+        out_shape=jax.ShapeDtypeStruct((width, length), f32),
+        in_specs=[pl.BlockSpec(memory_space=pltpu.HBM)],
+        out_specs=pl.BlockSpec(memory_space=pltpu.HBM),
+        scratch_shapes=[dma((PIECES,))],
+    )(result)
+
+
+def deliver(source, target, sem):
+    rows = source.shape[0] // PIECES
+    copies = [
+        pltpu.make_async_copy(
+            source.at[pl.ds(i * rows, rows), :], target.at[pl.ds(i * rows, rows), :], sem.at[i]
+        )
+        for i in range(PIECES)
+    ]
+    for copy in copies:
+        copy.start()
+    for copy in copies:
+        copy.wait()
 
 
 def fits(mesh, shape):

time: 47.8 us -> 62 us (1.30)
  Pallas kernels: 45.7 us -> 61.8 us
  local copies, waits for them, and re-layouts: 1.89 us -> 0 us
    pallas_call x0 -> x1, Pallas kernels: none -> 17.1 us  [fused(): pl.pallas_call(deliver, out_shape=jax.ShapeDtypeStruct((width, length), f...]
    unnamed x1 -> x0, local copies, waits for them, and re-layouts: 1.89 us -> none
    pallas_call x1, Pallas kernels: 45.7 us -> 44.8 us  [fused(): pl.pallas_call(functools.partial(kernel, groups, atom_count * lax.axis_si...]
where the time goes in v6:
time: 62 us; the launch traced here: 61.8 us
  Pallas kernels  61.8 us (100%)
    pallas_call x1, Pallas kernels, fused(): pl.pallas_call(functools.partial(kernel, groups, atom_count * lax.axis_si...  44.8 us
    pallas_call x1, Pallas kernels, fused(): pl.pallas_call(deliver, out_shape=jax.ShapeDtypeStruct((width, length), f...  17.1 us

profile of v6, /device:TPU:0, one launch (start us, length us, event | category | flops | bytes accessed | tf_op | source)
XLA Modules:
  0.0 61.8 jit_solution(323484224397021867)
XLA Ops:
  0.0 44.8 %shard_map.28.source = f32[128,1024]{1,0:T(8,128)} custom-call(f32[3,64,2048]{2,1,0:T(8,128)} %bitcast.1, bf16[2848,256]{1,0:T(8,128)(2,1)} %constant.2.clone.table), custom_call_target="tpu_custom_call" | custom-call | tf_op jit(solution)/shard_map/pallas_call | solution.py:394
  44.8 17.1 %shard_map.29 = f32[128,1024]{1,0:T(8,128)} custom-call(f32[128,1024]{1,0:T(8,128)} %shard_map.28.source), custom_call_target="tpu_custom_call" | custom-call | tf_op jit(solution)/shard_map/pallas_call | solution.py:420

commit v7 on v6

--- a/solution.py
+++ b/solution.py
@@ -13,7 +13,7 @@
 
 BLOCK = 256
 LANES = 128
-PIECES = 8
+PIECES = 4
 MESH = pl.DeviceIdType.MESH
 
 
@@ -422,21 +422,25 @@
         out_shape=jax.ShapeDtypeStruct((width, length), f32),
         in_specs=[pl.BlockSpec(memory_space=pltpu.HBM)],
         out_specs=pl.BlockSpec(memory_space=pltpu.HBM),
-        scratch_shapes=[dma((PIECES,))],
+        scratch_shapes=[pltpu.VMEM((width, length), f32), dma((PIECES,)), dma((PIECES,))],
     )(result)
 
 
-def deliver(source, target, sem):
+def deliver(source, target, held, come, go):
     rows = source.shape[0] // PIECES
-    copies = [
-        pltpu.make_async_copy(
-            source.at[pl.ds(i * rows, rows), :], target.at[pl.ds(i * rows, rows), :], sem.at[i]
-        )
-        for i in range(PIECES)
+    here = [pl.ds(i * rows, rows) for i in range(PIECES)]
+    inward = [
+        pltpu.make_async_copy(source.at[at, :], held.at[at, :], come.at[i]) for i, at in enumerate(here)
     ]
-    for copy in copies:
+    outward = [
+        pltpu.make_async_copy(held.at[at, :], target.at[at, :], go.at[i]) for i, at in enumerate(here)
+    ]
+    for copy in inward:
         copy.start()
-    for copy in copies:
+    for before, after in zip(inward, outward):
+        before.wait()
+        after.start()
+    for copy in outward:
         copy.wait()
 
 

time: 62 us -> 46.7 us (0.75)
  Pallas kernels: 61.8 us -> 46.6 us
    pallas_call x1, Pallas kernels: 17.1 us -> 1.82 us  [fused(): pl.pallas_call(deliver, out_shape=jax.ShapeDtypeStruct((width, length), f...]
where the time goes in v7:
time: 46.7 us; the launch traced here: 46.6 us
  Pallas kernels  46.6 us (100%)
    pallas_call x1, Pallas kernels, fused(): pl.pallas_call(functools.partial(kernel, groups, atom_count * lax.axis_si...  44.8 us
    pallas_call x1, Pallas kernels, fused(): pl.pallas_call(deliver, out_shape=jax.ShapeDtypeStruct((width, length), f...  1.82 us

profile of v7, /device:TPU:0, one launch (start us, length us, event | category | flops | bytes accessed | tf_op | source)
XLA Modules:
  0.0 46.6 jit_solution(6344064690308996701)
XLA Ops:
  0.0 44.8 %shard_map.28.source = f32[128,1024]{1,0:T(8,128)} custom-call(f32[3,64,2048]{2,1,0:T(8,128)} %bitcast.1, bf16[2848,256]{1,0:T(8,128)(2,1)} %constant.2.clone.table), custom_call_target="tpu_custom_call" | custom-call | tf_op jit(solution)/shard_map/pallas_call | solution.py:394
  44.8 1.8 %shard_map.29 = f32[128,1024]{1,0:T(8,128)} custom-call(f32[128,1024]{1,0:T(8,128)} %shard_map.28.source), custom_call_target="tpu_custom_call" | custom-call | tf_op jit(solution)/shard_map/pallas_call | solution.py:420

commit v8 on v6

--- a/solution.py
+++ b/solution.py
@@ -13,7 +13,6 @@
 
 BLOCK = 256
 LANES = 128
-PIECES = 8
 MESH = pl.DeviceIdType.MESH
 
 
@@ -108,7 +107,7 @@
     sums = [col <= row, col >= row, col <= BLOCK - 1 - row]
     pieces = rounded(forward, 2)
     pieces += [part.astype(ml_dtypes.bfloat16) for part in sums]
-    pieces += [part for pair in zip(*(rounded(half, 2) for half in inverse)) for part in pair]
+    pieces += [part for pair in zip(*(rounded(half, 3) for half in inverse)) for part in pair]
     return np.concatenate(pieces, axis=0)
 
 
@@ -391,7 +390,7 @@
     lanes = -(-3 * frames // LANES) * LANES
     f32, bf16 = jnp.float32, jnp.bfloat16
     dma = pltpu.SemaphoreType.DMA
-    result = pl.pallas_call(
+    return pl.pallas_call(
         functools.partial(kernel, groups, atom_count * lax.axis_size("atoms")),
         out_shape=jax.ShapeDtypeStruct((width, length), f32),
         in_specs=[pl.BlockSpec(memory_space=pltpu.HBM)] * 2,
@@ -414,30 +413,9 @@
             dma, dma, dma((groups,)), dma((groups,)),
         ],
         compiler_params=pltpu.CompilerParams(
-            collective_id=0, has_side_effects=True, vmem_limit_bytes=60 * 1024 * 1024
+            collective_id=0, has_side_effects=True, vmem_limit_bytes=61_190_000
         ),
     )(jnp.transpose(displacements, (1, 0, 2)), jnp.asarray(table))
-    return pl.pallas_call(
-        deliver,
-        out_shape=jax.ShapeDtypeStruct((width, length), f32),
-        in_specs=[pl.BlockSpec(memory_space=pltpu.HBM)],
-        out_specs=pl.BlockSpec(memory_space=pltpu.HBM),
-        scratch_shapes=[dma((PIECES,))],
-    )(result)
-
-
-def deliver(source, target, sem):
-    rows = source.shape[0] // PIECES
-    copies = [
-        pltpu.make_async_copy(
-            source.at[pl.ds(i * rows, rows), :], target.at[pl.ds(i * rows, rows), :], sem.at[i]
-        )
-        for i in range(PIECES)
-    ]
-    for copy in copies:
-        copy.start()
-    for copy in copies:
-        copy.wait()
 
 
 def fits(mesh, shape):

time: 62 us -> 46.8 us (0.75)
  Pallas kernels: 61.8 us -> 44.8 us
  local copies, waits for them, and re-layouts: 0 us -> 1.89 us
    pallas_call x1 -> x0, Pallas kernels: 17.1 us -> none  [fused(): pl.pallas_call(deliver, out_shape=jax.ShapeDtypeStruct((width, length), f...]
    unnamed x0 -> x1, local copies, waits for them, and re-layouts: none -> 1.89 us
where the time goes in v8:
time: 46.8 us; the launch traced here: 46.7 us
  Pallas kernels  44.8 us (96%)
  local copies, waits for them, and re-layouts  1.89 us (4%)
    pallas_call x1, Pallas kernels, fused(): pl.pallas_call(functools.partial(kernel, groups, atom_count * lax.axis_si...  44.8 us
    unnamed x1, local copies, waits for them, and re-layouts  1.89 us

profile of v8, /device:TPU:0, one launch (start us, length us, event | category | flops | bytes accessed | tf_op | source)
XLA Modules:
  0.0 46.7 jit_solution(10132667182248818728)
XLA Ops:
  0.0 44.8 %shard_map.28 = f32[128,1024]{1,0:T(8,128)} custom-call(f32[3,64,2048]{2,1,0:T(8,128)} %bitcast.1, bf16[3360,256]{1,0:T(8,128)(2,1)} %constant.2.clone.table), custom_call_target="tpu_custom_call" | custom-call | tf_op jit(solution)/shard_map/pallas_call | solution.py:393
  44.8 1.9 %copy.4 = f32[128,1024]{1,0:T(8,128)} copy(f32[128,1024]{1,0:T(8,128)} %shard_map.28) | data formatting | bytes 1048576

commit v9 on v7

--- a/solution.py
+++ b/solution.py
@@ -135,8 +135,8 @@
 
 
 def kernel(
-    groups, atom_total, x, table, out,
-    xv, recv, mine, sibling, total, msgs, held, drift, spectrum, acc_re, acc_im, acc_top, squares,
+    groups, atom_total, x, table, result_out,
+    out, out_sem, xv, recv, mine, sibling, total, msgs, held, drift, spectrum, acc_re, acc_im, acc_top, squares,
     load_sem, const_sem, own_sem, send_sem, recv_sem, pair_send, pair_recv, msg_send, msg_recv,
 ):
     me, core = lax.axis_index("frames"), lax.axis_index("atoms")
@@ -371,14 +371,22 @@
             value = value + sums_of[j]
         whole.append(value)
     result = later + earlier + jnp.concatenate(whole, axis=1) + corr
+    leaving = []
     for i, piece in enumerate(lanes_of(result)):
         lag = i * BLOCK + lax.broadcasted_iota(jnp.int32, (BLOCK, 1), 0)
         pairs = (blocks * BLOCK - lag).astype(jnp.float32)
         out[:, i * BLOCK : (i + 1) * BLOCK] = jnp.transpose(piece / pairs)
+        leave = pltpu.make_async_copy(
+            out.at[:, pl.ds(i * BLOCK, BLOCK)], result_out.at[:, pl.ds(i * BLOCK, BLOCK)], out_sem.at[i]
+        )
+        leave.start()
+        leaving.append(leave)
 
     for c in range(3):
         sent(c, False)
         sent(c, True)
+    for leave in leaving:
+        leave.wait()
 
 
 def fused(displacements):
@@ -395,8 +403,10 @@
         functools.partial(kernel, groups, atom_count * lax.axis_size("atoms")),
         out_shape=jax.ShapeDtypeStruct((width, length), f32),
         in_specs=[pl.BlockSpec(memory_space=pltpu.HBM)] * 2,
-        out_specs=pl.BlockSpec(memory_space=pltpu.VMEM),
+        out_specs=pl.BlockSpec(memory_space=pltpu.HBM),
         scratch_shapes=[
+            pltpu.VMEM((width, length), f32),
+            dma((blocks,)),
             pltpu.VMEM((3, frames, atom_count), f32),
             pltpu.VMEM((3, length, width), f32),
             pltpu.VMEM((1, lanes), f32),

time: 46.7 us -> 46.7 us (level)
  no operation moved by 1% of the time
where the time goes in v9:
time: 46.7 us; the launch traced here: 46.6 us
  Pallas kernels  46.5 us (100%)
    pallas_call x1, Pallas kernels, fused(): pl.pallas_call(functools.partial(kernel, groups, atom_count * lax.axis_si...  44.7 us
    pallas_call x1, Pallas kernels, fused(): pl.pallas_call(deliver, out_shape=jax.ShapeDtypeStruct((width, length), f...  1.82 us

profile of v9, /device:TPU:0, one launch (start us, length us, event | category | flops | bytes accessed | tf_op | source)
XLA Modules:
  0.0 46.6 jit_solution(12837758025230435451)
XLA Ops:
  0.0 44.7 %shard_map.28.source = f32[128,1024]{1,0:T(8,128)} custom-call(f32[3,64,2048]{2,1,0:T(8,128)} %bitcast.1, bf16[2848,256]{1,0:T(8,128)(2,1)} %constant.2.clone.table), custom_call_target="tpu_custom_call" | custom-call | tf_op jit(solution)/shard_map/pallas_call | solution.py:402
  44.7 1.8 %shard_map.29 = f32[128,1024]{1,0:T(8,128)} custom-call(f32[128,1024]{1,0:T(8,128)} %shard_map.28.source), custom_call_target="tpu_custom_call" | custom-call | tf_op jit(solution)/shard_map/pallas_call | solution.py:430
